TPU v7x, 128 devices: a whole 4x4x4 slice. The times are simulated.
128 devices in a mesh: dp: 2 (over y_lo), out: 16 (over x, z), in: 4 (over y_hi, core).
Axes of the slice: x: 4, y: 4 (y_hi: 2, y_lo: 2; y = y_hi * 2 + y_lo), z: 4, core: 2. Of those that a mesh axis runs over, the one named last changes fastest.
Arguments:
- features: bfloat16 [3072, 6144], P('dp', 'in'), may hold values from -6 to 6
- grad_qkv: bfloat16 [3072, 18432], P(('dp', 'in'), 'out'), may hold values from -0.47851562 to 0.47851562
- grad_act: bfloat16 [3072, 24576], P(('dp', 'in'), 'out'), may hold values from -0.47851562 to 0.47851562
- preact: bfloat16 [3072, 24576], P(('dp', 'in'), 'out'), may hold values from -9 to 9
- w_qkv: bfloat16 [6144, 18432], P('in', 'out'), may hold values from -0.078125 to 0.078125
- w_mlp: bfloat16 [6144, 24576], P('in', 'out'), may hold values from -0.078125 to 0.078125
Outputs:
- grad_features: bfloat16 [3072, 6144], P(('dp', 'out'), 'in')
- grad_wqkv: bfloat16 [6144, 18432], P('in', 'out')
- grad_wmlp: bfloat16 [6144, 24576], P('in', 'out')
All inputs are finite; a program needn't handle non-finite values.
Results may differ from a plain program's by a relative error of at most 0.0059.
Values may be sent and summed in bfloat16 or wider, within the bound.
A program may use at most 128 MiB of HBM per device.

v0:
```python
import math

import jax
import jax.numpy as jnp
from jax import lax
from jax.sharding import PartitionSpec as P


def gelu_slope(values):
    cumulative = 0.5 * (1.0 + lax.erf(values / math.sqrt(2.0)))
    density = jnp.exp(-0.5 * values * values) / math.sqrt(2.0 * math.pi)
    return cumulative + values * density


def rows_times(gathered, weight):
    return lax.dot_general(
        gathered, weight, (((1,), (1,)), ((), ())), preferred_element_type=jnp.float32
    )


def local(features, grad_qkv, grad_act, preact, w_qkv, w_mlp):
    derivative = gelu_slope(preact.astype(jnp.float32))
    grad_hidden = (grad_act.astype(jnp.float32) * derivative).astype(jnp.bfloat16)
    full_qkv, full_hidden = (
        lax.all_gather(grad_qkv, "in", axis=0, tiled=True),
        lax.all_gather(grad_hidden, "in", axis=0, tiled=True),
    )
    input_grad = lax.psum_scatter(
        rows_times(full_qkv, w_qkv) + rows_times(full_hidden, w_mlp),
        "out",
        scatter_dimension=0,
        tiled=True,
    )
    qkv_term = lax.dot_general(
        features, full_qkv, (((0,), (0,)), ((), ())), preferred_element_type=jnp.float32
    )
    mlp_term = lax.dot_general(
        features, full_hidden, (((0,), (0,)), ((), ())), preferred_element_type=jnp.float32
    )
    return (
        input_grad.astype(jnp.bfloat16),
        lax.psum(qkv_term.astype(jnp.bfloat16), "dp"),
        lax.psum(mlp_term.astype(jnp.bfloat16), "dp"),
    )


def solution(mesh):
    return jax.shard_map(
        local,
        mesh=mesh,
        in_specs=(
            P("dp", "in"),
            P(("dp", "in"), "out"),
            P(("dp", "in"), "out"),
            P(("dp", "in"), "out"),
            P("in", "out"),
            P("in", "out"),
        ),
        out_specs=(P(("dp", "out"), "in"), P("in", "out"), P("in", "out")),
        check_vma=False,
    )
```

profile of v0, /device:TPU:16, one launch (start us, length us, event | category | flops | bytes accessed | tf_op | source)
XLA Modules:
  0.0 408.5 jit_solution(17040425904923186547)
XLA Ops:
  7.2 0.0 copy-start
  7.2 0.0 all-gather.3.cloned.1.call-start
  7.2 0.7 all-gather.3.cloned.1.call-update
  7.9 0.0 all-gather.5.cloned.1.call-start
  8.0 3.5 fusion.8
  11.4 0.0 all-gather.5.cloned.1.call-update
  11.4 0.0 all-reduce.3.cloned.1.call-start
  11.5 32.5 %all-gather.3.cloned.1.call-done = bf16[1536,1152]{1,0:T(8,128)(2,1)} async-done(((bf16[384,1152]{1,0:T(8,128)(2,1)}), bf16[1536,1152]{1,0:T(8,128)(2,1)}) %all-gather.3.cloned.1.call-update) | async-done | bytes 3538960 | tf_op jit(solution)/shard_map/all_gather | solution.py:25
  44.0 10.5 %convolution_convert_fusion = bf16[1536,1152]{1,0:T(8,128)(2,1)} fusion(bf16[1536,1536]{1,0:T(8,128)(2,1)} %param.6, bf16[1536,1152]{1,0:T(8,128)(2,1)} %all-gather.3.cloned.1.call-done), kind=kOutput, calls=%fused_computation.1 | convolution fusion | flops 5437587456 | bytes 11796480 | tf_op jit(solution)/shard_map/dot_general | solution.py:34
  54.5 32.7 %all-gather.5.cloned.1.call-done = bf16[1536,1536]{1,0:T(8,128)(2,1)} async-done(((bf16[384,1536]{1,0:T(8,128)(2,1)}), bf16[1536,1536]{1,0:T(8,128)(2,1)}) %all-gather.5.cloned.1.call-update) | async-done | bytes 4718608 | tf_op jit(solution)/shard_map/all_gather | solution.py:26
  87.2 12.3 %fusion = bf16[1536,1536]{0,1:T(8,128)(2,1)} fusion(bf16[1536,1536]{1,0:T(8,128)(2,1)} %all-gather.5.cloned.1.call-done, bf16[1536,1536]{1,0:T(8,128)(2,1)} %param.6), kind=kOutput, calls=%fused_computation.3 | convolution fusion | flops 7250116608 | bytes 14155776 | tf_op jit(solution)/shard_map/dot_general | solution.py:37
  99.5 0.0 all-reduce.3.cloned.1.call-update
  99.5 0.2 reduce-scatter.2.cloned.1.call-start
  99.7 0.0 copy-start.1
  99.7 11.0 %fusion.9 = f32[1536,1536]{1,0:T(8,128)S(1)} fusion(bf16[1536,1536]{1,0:T(8,128)(2,1)} %all-gather.5.cloned.1.call-done, bf16[1536,1536]{1,0:T(8,128)(2,1)} %param.11), kind=kOutput, calls=%fused_computation.16 | convolution fusion | flops 7247757312 | bytes 18874368 | tf_op jit(solution)/shard_map/dot_general | solution.py:16
  110.8 0.0 copy-done
  110.8 0.0 copy-done.1
  110.8 9.2 %convolution_add_fusion = f32[1536,1536]{1,0:T(8,128)} fusion(f32[1536,1536]{1,0:T(8,128)S(1)} %fusion.9, bf16[1536,1152]{1,0:T(8,128)(2,1)S(1)} %copy-done.1, bf16[1536,1152]{1,0:T(8,128)(2,1)S(1)} %copy-done), kind=kOutput, calls=%fused_computation | convolution fusion | flops 5438177280 | bytes 25952256 | tf_op jit(solution)/shard_map/dot_general | solution.py:16
  120.0 0.0 reduce-scatter.2.cloned.1.call-update
  120.0 183.8 %all-reduce.3.cloned.1.call-done = (bf16[1536,1152]{1,0:T(8,128)(2,1)}, bf16[1536,1536]{0,1:T(8,128)(2,1)}) async-done(((bf16[1536,1152]{1,0:T(8,128)(2,1)}, bf16[1536,1536]{0,1:T(8,128)(2,1)}), (bf16[1536,1152]{1,0:T(8,128)(2,1)}, bf16[1536,1536]{0,1:T(8,128)(2,1)})) %all-reduce.3.cloned.1.call-update) | async-done | bytes 8257552 | tf_op jit(solution)/shard_map/psum | solution.py:42
  303.8 6.6 %copy.9 = bf16[1536,1536]{1,0:T(8,128)(2,1)} copy(bf16[1536,1536]{0,1:T(8,128)(2,1)} %get-tuple-element.7) | data formatting | bytes 9437184
  310.4 85.6 %reduce-scatter.2.cloned.1.call-done = f32[96,1536]{1,0:T(8,128)} async-done(((f32[1536,1536]{1,0:T(8,128)}), f32[96,1536]{1,0:T(8,128)}) %reduce-scatter.2.cloned.1.call-update) | async-done | bytes 589840 | tf_op jit(solution)/shard_map/reduce_scatter | solution.py:28
  396.1 1.8 convert_element_type.24
  397.9 4.1 copy.12
Async XLA Ops:
  7.2 103.6 %copy-start = (bf16[1536,1152]{1,0:T(8,128)(2,1)S(1)}, bf16[1536,1152]{1,0:T(8,128)(2,1)}, u32[]{:S(2)}) copy-start(bf16[1536,1152]{1,0:T(8,128)(2,1)} %param.10) | copy-start | bytes 10616836
  7.2 36.8 %all-gather.3.cloned.1.call-start = ((), (), s32[]{:S(2)}) async-start(), calls=%async_computation.1 | async-start | bytes 4423680 | tf_op jit(solution)/shard_map/all_gather | solution.py:25
  7.9 79.3 %all-gather.5.cloned.1.call-start = ((), (), s32[]{:S(2)}) async-start(), calls=%async_computation.2 | async-start | bytes 5898240 | tf_op jit(solution)/shard_map/all_gather | solution.py:26
  11.4 292.4 %all-reduce.3.cloned.1.call-start = ((), (), s32[]{:S(2)}) async-start(), calls=%async_computation.4 | async-start | bytes 16515072 | tf_op jit(solution)/shard_map/psum | solution.py:42
  99.5 296.6 %reduce-scatter.2.cloned.1.call-start = ((), (), s32[]{:S(2)}) async-start(), calls=%async_computation.3 | async-start | bytes 10027008 | tf_op jit(solution)/shard_map/reduce_scatter | solution.py:28
  99.7 11.0 %copy-start.1 = (bf16[1536,1152]{1,0:T(8,128)(2,1)S(1)}, bf16[1536,1152]{1,0:T(8,128)(2,1)}, u32[]{:S(2)}) copy-start(bf16[1536,1152]{1,0:T(8,128)(2,1)} %all-gather.3.cloned.1.call-done) | copy-start | bytes 10616836
Sparse Core Ops, SparseCore 0:
  9.7 34.2 all-gather.2
  46.2 40.9 all-gather.4
  99.6 204.1 all-reduce.2
  307.2 88.8 reduce-scatter.1
where the time goes:
time: 409 us; the launch traced here: 408 us
  waiting for transfers between devices  335 us (82%)
  matrix products  43 us (11%)
  between operations  13.8 us (3%)
  local copies, waits for them, and re-layouts  10.7 us (3%)
  other arithmetic  5.26 us (1%)
    psum x1, waiting for transfers between devices, local(): lax.psum(qkv_term.astype(jnp.bfloat16), 'dp')  184 us
    reduce_scatter x1, waiting for transfers between devices, local(): lax.psum_scatter(rows_times(full_qkv, w_qkv) + rows_times(full_hidden, w_...  85.6 us
    all_gather x1, waiting for transfers between devices, local(): lax.all_gather(grad_hidden, 'in', axis=0, tiled=True)  32.7 us
    all_gather x1, waiting for transfers between devices, local(): lax.all_gather(grad_qkv, 'in', axis=0, tiled=True)  32.5 us
    dot_general x2, matrix products, rows_times(): lax.dot_general(gathered, weight, (((1,), (1,)), ((), ())), preferred_ele...  20.2 us
    dot_general x1, matrix products, local(): lax.dot_general(features, full_hidden, (((0,), (0,)), ((), ())), preferre...  12.3 us
    unnamed x6, local copies, waits for them, and re-layouts  10.7 us
    dot_general x1, matrix products, local(): lax.dot_general(features, full_qkv, (((0,), (0,)), ((), ())), preferred_e...  10.5 us
  transfers between devices with their start and end apart: 4, of which 4 were waited for; matrix products, arithmetic and copies ran while one was open for 10% of the time, Pallas kernels for 0%

commit v1 on v0

v1 whole, which is shorter than its diff:
```python
import math

import jax
import jax.numpy as jnp
from jax import lax
from jax.experimental import pallas as pl
from jax.experimental.pallas import tpu as pltpu
from jax.sharding import PartitionSpec as P

MESH = pl.DeviceIdType.MESH
BF = jnp.bfloat16
F32 = jnp.float32
NQ, NM, F = 1152, 1536, 1536
COLS = ((0, 0, 512), (0, 512, 512), (0, 1024, 128), (1, 0, 512), (1, 512, 512), (1, 1024, 512))


def gelu_slope(values):
    cumulative = 0.5 * (1.0 + lax.erf(values * (1.0 / math.sqrt(2.0))))
    density = jnp.exp(-0.5 * values * values) * (1.0 / math.sqrt(2.0 * math.pi))
    return cumulative + values * density


def kernel(feat, gq, ga, pre, wq_hbm, wm_hbm, gf_out, oq_hbm, om_hbm,
           Gq, Gm, FT, FTo, Wq, Wm, Pp, ra, rb, rx1, rx2, piece, stg, gout, aq, am,
           ssem, rsem, lsem):
    dp, o, i = lax.axis_index("dp"), lax.axis_index("out"), lax.axis_index("in")
    hi, core = i // 2, i % 2
    x, z = o // 4, o % 4
    same = 1 - (dp + core) % 2
    hiA = same * hi + (1 - same) * (1 - hi)
    hiB = 1 - hiA
    p1 = (hiB + core) % 2
    devA = (1 - dp, o, 2 * hiA + core)
    devB = (1 - dp, o, 2 * hiB + core)
    sib = (dp, o, 2 * hi + 1 - core)
    partner = (1 - dp, o, i)

    def at(xx, zz):
        return ((xx + 4) % 4) * 4 + (zz + 4) % 4

    def plane(xx, zz):
        return (dp, at(xx, zz), i)

    G, W, ACC, OUT = (Gq, Gm), (Wq, Wm), (aq, am), (oq_hbm, om_hbm)

    ids = {}
    sent = []

    def rc(key, src, dst, dev):
        n = ids.setdefault(key, len(ids))
        return pltpu.make_async_remote_copy(src_ref=src, dst_ref=dst, send_sem=ssem.at[n], recv_sem=rsem.at[n],
                                            device_id=dev, device_id_type=MESH)

    def send(key, src, dst, dev, when=None):
        c = rc(key, src, dst, dev)
        if when is None:
            c.start()
        else:
            pl.when(when)(c.start)
        sent.append((c, when))

    def got(key, dst):
        rc(key, dst, dst, sib).wait_recv()

    lids = {}
    lwait = {}

    def local(key, src, dst):
        n = lids.setdefault(key, len(lids))
        c = pltpu.make_async_copy(src, dst, lsem.at[n])
        c.start()
        lwait[key] = c

    for c in range(3):
        local(("ga", c), ga.at[:, c], stg.at[0, c])
        local(("pre", c), pre.at[:, c], stg.at[1, c])
        if c == 0:
            for b in range(4):
                for cc in range(3):
                    local(("f", b, cc), feat.at[b, :, cc], Pp.at[b // 2, cc, b % 2])
    for c in range(3):
        local(("q", c), gq.at[:, c], Gq.at[0, c, core])
    local(("wq",), wq_hbm, Wq)
    local(("wm",), wm_hbm, Wm)

    bar = pltpu.get_barrier_semaphore()
    friends = (devA, devB, sib, plane(x + 1, z), plane(x - 1, z), plane(x, z + 1), plane(x, z - 1))
    for d in friends:
        pl.semaphore_signal(bar, inc=1, device_id=d, device_id_type=MESH)
    pl.semaphore_wait(bar, len(friends))

    def tok(k, slot, c, pos):
        return G[k].at[slot, c, pos]

    def own_q(c):
        send(("y1", 0, c), gq.at[:, c], tok(0, 1, c, hi), devA)
        send(("s0", 0, c), gq.at[:, c], tok(0, 0, c, core), sib)

    def own_m(c):
        lwait["ga", c].wait()
        lwait["pre", c].wait()

        def body(j, carry):
            a = stg[0, c, j].astype(F32)
            v = stg[1, c, j].astype(F32)
            Gm[0, c, core, j] = (a * gelu_slope(v)).astype(BF)
            return carry

        lax.fori_loop(0, 4, body, 0)
        send(("y1", 1, c), tok(1, 0, c, core), tok(1, 1, c, hi), devA)
        send(("s0", 1, c), tok(1, 0, c, core), tok(1, 0, c, core), sib)

    def Y1(c):
        for k in (0, 1):
            here = tok(k, 1, c, hiB)
            got(("y1", k, c), here)
            send(("y2", k, c), here, tok(k, 2, c, core), devA)
            send(("s1", k, c), here, here, sib)

    def Y2(c):
        for k in (0, 1):
            here = tok(k, 2, c, core)
            got(("y2", k, c), here)
            send(("s2", k, c), here, here, sib)

    def SIB(slot, c):
        pos = {0: 1 - core, 1: 1 - hiB, 2: 1 - core}[slot]
        for k in (0, 1):
            got(("s%d" % slot, k, c), tok(k, slot, c, pos))

    def col(n, slot, pos):
        k, c0, w = COLS[n]
        return G[k].at[slot, :, pos, :, :, pl.ds(c0, w)]

    def SEND3(n):
        send(("y3", n), col(n, 0, core), col(n, 3, hi), devB)

    def Y3(n):
        here = col(n, 3, hiA)
        got(("y3", n), here)
        send(("s3", n), here, here, sib)

    def SIB3(n):
        got(("s3", n), col(n, 3, 1 - hiA))

    def transpose():
        for b in range(4):
            for c in range(3):
                lwait["f", b, c].wait()
                h, p = b // 2, b % 2
                v = Pp[h, c, p].reshape(128, F)
                FT[h, :, c * 256 + p * 128:c * 256 + p * 128 + 128] = v.T
        rows = pl.ds(pl.multiple_of(o * 96, 32), 96)
        for b in range(4):
            h, p = b // 2, b % 2
            for c in range(3):
                piece[(h + p) % 2, :, c * 256 + h * 128:c * 256 + h * 128 + 128] = FT[h, rows, c * 256 + p * 128:c * 256 + p * 128 + 128]
        for p in (0, 1):
            send(("fp", p), piece.at[p], rows_of(p, o), partner)

    def rows_of(p, out, first=0, n=96):
        return FTo.at[p, pl.ds(pl.multiple_of(out * 96 + first, 16), n), :]

    def on(p, da, db):
        return at(x + da, z + db) if p == 0 else at(x + db, z + da)

    def to(p, da, db):
        return (dp, on(p, da, db), i)

    def F0():
        for p in (0, 1):
            here = rows_of(p, o)
            got(("fp", p), here)
            send(("f1", p, 0), here, here, to(p, 1, 0))
            send(("f1", p, 1), here, here, to(p, -1, 0))

    OFF = (0, -1, 1, 2)

    def spread(p, k):
        here = rows_of(p, on(p, OFF[k], 0))
        send(("f2", p, k, 0), here, here, to(p, 0, 1))
        send(("f2", p, k, 1), here, here, to(p, 0, -1))

    def F1():
        for p in (0, 1):
            got(("f1", p, 0), rows_of(p, on(p, -1, 0)))
            half = rows_of(p, on(p, -1, 0), 0, 48)
            send(("f1", p, 2), half, half, to(p, 1, 0))
            got(("f1", p, 1), rows_of(p, on(p, 1, 0)))
            half = rows_of(p, on(p, 1, 0), 48, 48)
            send(("f1", p, 3), half, half, to(p, -1, 0))
        for k in (0, 1, 2):
            for p in (0, 1):
                spread(p, k)

    def F2():
        for p in (0, 1):
            got(("f1", p, 2), rows_of(p, on(p, 2, 0), 0, 48))
            got(("f1", p, 3), rows_of(p, on(p, 2, 0), 48, 48))
            spread(p, 3)

    def F3(k):
        for p in (0, 1):
            side = 0 if k < 2 else 1
            here = rows_of(p, on(p, OFF[k], -1 if side == 0 else 1))
            got(("f2", p, k, side), here)
            send(("f3", p, k), here, here, to(p, 0, 1 if side == 0 else -1))

    def F4():
        for p in (0, 1):
            for k in range(4):
                side = 1 if k < 2 else 0
                got(("f2", p, k, side), rows_of(p, on(p, OFF[k], -1 if side == 0 else 1)))
                got(("f3", p, k), rows_of(p, on(p, OFF[k], 2)))

    def GF(s, c):
        slot = 2 * s
        a = Gq[slot, c].reshape(256, NQ)
        b = Gm[slot, c].reshape(256, NM)
        r = lax.dot_general(a, Wq[...], (((1,), (1,)), ((), ())), preferred_element_type=F32)
        r = r + lax.dot_general(b, Wm[...], (((1,), (1,)), ((), ())), preferred_element_type=F32)
        Pp[s, c] = r.astype(BF).reshape(2, 4, 32, F)

    zl, zr, z2 = (z + 3) % 4, (z + 1) % 4, (z + 2) % 4
    A, B = pl.ds(0, 768), pl.ds(768, 768)

    def role(s):
        h = hi if s == 0 else 1 - hi
        is_d = (x // 2) == h
        odd = x % 2
        keep = jnp.where(is_d, odd, 1 - odd)
        return is_d, odd, keep

    def R1(s, c):
        send(("r1", s, c, 0), Pp.at[s, c, :, z2, :, A], ra.at[s, c, 0], plane(x, z + 1))
        send(("r1", s, c, 1), Pp.at[s, c, :, z2, :, B], ra.at[s, c, 1], plane(x, z - 1))

    def R2(s, c):
        got(("r1", s, c, 0), ra.at[s, c, 0])
        Pp[s, c, :, zr, :, 0:768] = (Pp[s, c, :, zr, :, 0:768].astype(F32) + ra[s, c, 0].astype(F32)).astype(BF)
        send(("r2", s, c, 0), Pp.at[s, c, :, zr], rb.at[s, c, 0], plane(x, z + 1))
        got(("r1", s, c, 1), ra.at[s, c, 1])
        Pp[s, c, :, zl, :, 768:1536] = (Pp[s, c, :, zl, :, 768:1536].astype(F32) + ra[s, c, 1].astype(F32)).astype(BF)
        send(("r2", s, c, 1), Pp.at[s, c, :, zl], rb.at[s, c, 1], plane(x, z - 1))

    def R3(s, c):
        is_d, odd, keep = role(s)
        got(("r2", s, c, 0), rb.at[s, c, 0])
        got(("r2", s, c, 1), rb.at[s, c, 1])
        v = Pp[s, c, :, z].astype(F32) + rb[s, c, 0].astype(F32) + rb[s, c, 1].astype(F32)
        Pp[s, c, :, z] = v.astype(BF)
        send(("r3", s, c), Pp.at[s, c, 1 - keep, z], rx1.at[s, c], plane(x + 1 - 2 * odd, z))

    def R4(s, c):
        is_d, odd, keep = role(s)
        got(("r3", s, c), rx1.at[s, c])
        Pp[s, c, keep, z] = (Pp[s, c, keep, z].astype(F32) + rx1[s, c].astype(F32)).astype(BF)
        send(("r4", s, c), Pp.at[s, c, keep, z], rx2.at[s, c], plane(x - 1 + 2 * odd, z), when=jnp.logical_not(is_d))

    def R5(s, c):
        is_d, odd, keep = role(s)

        @pl.when(is_d)
        def _():
            got(("r4", s, c), rx2.at[s, c])
            gout[c] = (Pp[s, c, keep, z].astype(F32) + rx2[s, c].astype(F32)).astype(BF)

    def PASS(slot, n):
        k, c0, w = COLS[n]
        f = (FT.at[hi], FTo.at[p1], FT.at[1 - hi], FTo.at[1 - p1])[slot]
        acc = ACC[k]
        step = min(w, 256)

        def body(j, carry):
            cs = pl.ds(pl.multiple_of(c0 + j * step, 128), step)
            g = G[k][slot, :, :, :, :, cs].reshape(768, step)
            r = jnp.dot(f[...], g, preferred_element_type=F32)
            if slot == 0:
                acc[:, cs] = r
            elif slot < 3:
                acc[:, cs] += r
            else:
                W[k][:, cs] = (acc[:, cs] + r).astype(BF)
            return carry

        lax.fori_loop(0, w // step, body, 0)
        if slot == 3:
            local(("o", n), W[k].at[:, pl.ds(c0, w)], OUT[k].at[:, pl.ds(c0, w)])

    own_q(0)
    own_m(0)
    own_q(1)
    transpose()
    own_m(1)
    own_q(2)
    own_m(2)
    for c in range(3):
        lwait["q", c].wait()
    lwait["wq",].wait()
    lwait["wm",].wait()
    SIB(0, 0)
    GF(0, 0)
    F0()
    Y1(0)
    SIB(0, 1)
    GF(0, 1)
    F1()
    SIB(0, 2)
    GF(0, 2)
    F2()
    PASS(0, 0)
    Y1(1)
    R1(0, 0)
    PASS(0, 1)
    PASS(0, 2)
    F3(0)
    R1(0, 1)
    PASS(0, 3)
    R2(0, 0)
    F3(1)
    PASS(0, 4)
    F3(2)
    R1(0, 2)
    R2(0, 1)
    PASS(0, 5)
    Y1(2)
    F3(3)
    R3(0, 0)
    R2(0, 2)
    Y2(0)
    R3(0, 1)
    R4(0, 0)
    SIB(2, 0)
    GF(1, 0)
    R1(1, 0)
    R3(0, 2)
    R4(0, 1)
    R5(0, 0)
    SEND3(0)
    Y2(1)
    R4(0, 2)
    R5(0, 1)
    SIB(2, 1)
    GF(1, 1)
    R1(1, 1)
    R2(1, 0)
    SEND3(1)
    SEND3(2)
    R5(0, 2)
    Y2(2)
    for n in (3, 4, 5):
        SEND3(n)
    SIB(2, 2)
    GF(1, 2)
    R1(1, 2)
    R2(1, 1)
    R3(1, 0)
    PASS(2, 0)
    PASS(2, 1)
    R2(1, 2)
    R3(1, 1)
    R4(1, 0)
    PASS(2, 2)
    PASS(2, 3)
    R3(1, 2)
    R4(1, 1)
    R5(1, 0)
    Y3(0)
    PASS(2, 4)
    PASS(2, 5)
    R4(1, 2)
    R5(1, 1)
    Y3(1)
    F4()
    for c in range(3):
        SIB(1, c)
    PASS(1, 0)
    R5(1, 2)
    for c in range(3):
        local(("gf", c), gout.at[c], gf_out.at[c])
    PASS(1, 1)
    Y3(2)
    PASS(1, 2)
    PASS(1, 3)
    Y3(3)
    PASS(1, 4)
    PASS(1, 5)
    for n in range(6):
        if n >= 4:
            Y3(n)
        SIB3(n)
        PASS(3, n)
    for n in range(6):
        lwait["o", n].wait()
    for c in range(3):
        lwait["gf", c].wait()
    for c, when in sent:
        if when is None:
            c.wait_send()
        else:
            pl.when(when)(c.wait_send)


def local(features, grad_qkv, grad_act, preact, w_qkv, w_mlp):
    shape = jax.ShapeDtypeStruct
    vm = pltpu.VMEM
    gf, gwq, gwm = pl.pallas_call(
        kernel,
        name="joined_projection_backward",
        out_shape=(shape((3, 32, F), BF), shape((F, NQ), BF), shape((F, NM), BF)),
        in_specs=[pl.BlockSpec(memory_space=pl.ANY)] * 6,
        out_specs=(pl.BlockSpec(memory_space=pl.ANY),) * 3,
        scratch_shapes=[
            vm((4, 3, 2, 4, 32, NQ), BF),
            vm((4, 3, 2, 4, 32, NM), BF),
            vm((2, F, 768), BF),
            vm((2, F, 768), BF),
            vm((F, NQ), BF),
            vm((F, NM), BF),
            vm((2, 3, 2, 4, 32, F), BF),
            vm((2, 3, 2, 2, 32, 768), BF),
            vm((2, 3, 2, 2, 32, F), BF),
            vm((2, 3, 32, F), BF),
            vm((2, 3, 32, F), BF),
            vm((2, 96, 768), BF),
            vm((2, 3, 4, 32, NM), BF),
            vm((3, 32, F), BF),
            vm((F, NQ), F32),
            vm((F, NM), F32),
            pltpu.SemaphoreType.DMA((112,)),
            pltpu.SemaphoreType.DMA((112,)),
            pltpu.SemaphoreType.DMA((32,)),
        ],
        compiler_params=pltpu.CompilerParams(collective_id=0, has_side_effects=True, vmem_limit_bytes=64 * 2**20 - 2**16),
        cost_estimate=pl.CostEstimate(flops=38_000_000_000, bytes_accessed=25_000_000, transcendentals=1_200_000),
    )(
        features.reshape(4, 4, 3, 32, F),
        grad_qkv.reshape(4, 3, 32, NQ),
        grad_act.reshape(4, 3, 32, NM),
        preact.reshape(4, 3, 32, NM),
        w_qkv,
        w_mlp,
    )
    return gf.reshape(96, F), gwq, gwm


def solution(mesh):
    return jax.shard_map(
        local,
        mesh=mesh,
        in_specs=(
            P("dp", "in"),
            P(("dp", "in"), "out"),
            P(("dp", "in"), "out"),
            P(("dp", "in"), "out"),
            P("in", "out"),
            P("in", "out"),
        ),
        out_specs=(P(("dp", "out"), "in"), P("in", "out"), P("in", "out")),
        check_vma=False,
    )
```

time: 409 us -> 131 us (0.32)
  waiting for transfers between devices: 335 us -> 0 us
  Pallas kernels: 0 us -> 122 us
  matrix products: 43 us -> 0 us
  between operations: 13.8 us -> 0.64 us
  other arithmetic: 5.26 us -> 0 us
    psum x1 -> x0, waiting for transfers between devices: 184 us -> none  [local(): lax.psum(qkv_term.astype(jnp.bfloat16), 'dp')]
    pallas_call x0 -> x1, Pallas kernels: none -> 122 us  [local(): pl.pallas_call(kernel, name='joined_projection_backward', out_shape=(shap...]
    reduce_scatter x1 -> x0, waiting for transfers between devices: 85.6 us -> none  [local(): lax.psum_scatter(rows_times(full_qkv, w_qkv) + rows_times(full_hidden, w_...]
    all_gather x2 -> x0, waiting for transfers between devices: 65.2 us -> none  [the longest x1 32.7 us: local(): lax.all_gather(grad_hidden, 'in', axis=0, tiled=True)]
    dot_general x4 -> x0, matrix products: 43 us -> none  [the longest x2 20.2 us: rows_times(): lax.dot_general(gathered, weight, (((1,), (1,)), ((), ())), preferred_ele...]
    convert_element_type x2 -> x0, other arithmetic: 5.26 us -> none  [the longest x1 3.46 us: local(): (grad_act.astype(jnp.float32) * derivative).astype(jnp.bfloat16)]
    unnamed x6 -> x5, local copies, waits for them, and re-layouts: 10.7 us -> 8.1 us
  transfers between devices with their start and end apart: 4 -> 0, of which waited for: 4 -> 0; matrix products, arithmetic and copies ran while one was open for 10% -> 0% of each run, Pallas kernels for 0% -> 0%
where the time goes in v1:
time: 131 us
  Pallas kernels  122 us (93%)
  local copies, waits for them, and re-layouts  8.1 us (6%)
    pallas_call x1, Pallas kernels, local(): pl.pallas_call(kernel, name='joined_projection_backward', out_shape=(shap...  122 us
    unnamed x5, local copies, waits for them, and re-layouts  8.1 us

profile of v1, /device:TPU:16, one launch (start us, length us, event | category | flops | bytes accessed | tf_op | source)
XLA Modules:
  0.0 131.0 jit_solution(9319786788771717907)
XLA Ops:
  0.6 122.2 %joined_projection_backward.1 = (bf16[3,32,1536]{2,1,0:T(8,128)(2,1)}, bf16[1536,1152]{1,0:T(8,128)(2,1)}, bf16[1536,1536]{1,0:T(8,128)(2,1)}) custom-call(bf16[4,4,3,32,1536]{4,3,2,1,0:T(8,128)(2,1)} %bitcast.6, bf16[4,3,32,1152]{3,2,1,0:T(8,128)(2,1)} %bitcast.9, bf16[4,3,32,1536]{3,2,1,0:T(8,128)(2,1)} %bitcast.7, bf16[4,3,32,1536]{3,2,1,0:T(8,128)(2,1)} %bitcast.8, ...), custom_call_target="tpu_custom_call" | custom-call | flops 38000001024 | bytes 25000000 | tf_op jit(solution)/shard_map/joined_projection_backward/pallas_call | solution.py:407
  122.9 1.7 %copy.12 = bf16[96,1536]{1,0:T(8,128)(2,1)} copy(bf16[96,1536]{1,0:T(8,128)(2,1)} %bitcast.5) | data formatting | bytes 589824
  124.6 0.0 copy-start
  124.6 4.2 %copy.13 = bf16[1536,1152]{1,0:T(8,128)(2,1)} copy(bf16[1536,1152]{1,0:T(8,128)(2,1)} %get-tuple-element.13) | data formatting | bytes 7077888
  128.8 0.0 copy-done
  128.8 2.2 %copy.14 = bf16[1536,1536]{1,0:T(8,128)(2,1)} copy(bf16[1536,1536]{1,0:T(8,128)(2,1)S(1)} %copy-done) | data formatting | bytes 9437184
Async XLA Ops:
  124.6 4.2 %copy-start = (bf16[1536,1536]{1,0:T(8,128)(2,1)S(1)}, bf16[1536,1536]{1,0:T(8,128)(2,1)}, u32[]{:S(2)}) copy-start(bf16[1536,1536]{1,0:T(8,128)(2,1)} %get-tuple-element.14) | copy-start | bytes 14155780

commit v2 on v1

--- a/solution.py
+++ b/solution.py
@@ -71,13 +71,12 @@
         c.start()
         lwait[key] = c
 
+    for b in range(4):
+        for c in range(3):
+            local(("f", b, c), feat.at[b, :, c], Pp.at[b // 2, c, b % 2])
     for c in range(3):
         local(("ga", c), ga.at[:, c], stg.at[0, c])
         local(("pre", c), pre.at[:, c], stg.at[1, c])
-        if c == 0:
-            for b in range(4):
-                for cc in range(3):
-                    local(("f", b, cc), feat.at[b, :, cc], Pp.at[b // 2, cc, b % 2])
     for c in range(3):
         local(("q", c), gq.at[:, c], Gq.at[0, c, core])
     local(("wq",), wq_hbm, Wq)
@@ -87,16 +86,21 @@
     friends = (devA, devB, sib, plane(x + 1, z), plane(x - 1, z), plane(x, z + 1), plane(x, z - 1))
     for d in friends:
         pl.semaphore_signal(bar, inc=1, device_id=d, device_id_type=MESH)
-    pl.semaphore_wait(bar, len(friends))
+
+    def friends_here():
+        pl.semaphore_wait(bar, len(friends))
 
     def tok(k, slot, c, pos):
         return G[k].at[slot, c, pos]
 
-    def own_q(c):
+    def own(c):
         send(("y1", 0, c), gq.at[:, c], tok(0, 1, c, hi), devA)
+        send(("y1", 1, c), tok(1, 0, c, core), tok(1, 1, c, hi), devA)
+
+    def sib_q(c):
         send(("s0", 0, c), gq.at[:, c], tok(0, 0, c, core), sib)
 
-    def own_m(c):
+    def slope(c):
         lwait["ga", c].wait()
         lwait["pre", c].wait()
 
@@ -107,7 +111,8 @@
             return carry
 
         lax.fori_loop(0, 4, body, 0)
-        send(("y1", 1, c), tok(1, 0, c, core), tok(1, 1, c, hi), devA)
+
+    def sib_m(c):
         send(("s0", 1, c), tok(1, 0, c, core), tok(1, 0, c, core), sib)
 
     def Y1(c):
@@ -132,8 +137,16 @@
         k, c0, w = COLS[n]
         return G[k].at[slot, :, pos, :, :, pl.ds(c0, w)]
 
-    def SEND3(n):
-        send(("y3", n), col(n, 0, core), col(n, 3, hi), devB)
+    def SEND3(n, light=None):
+        send(("y3", n), col(n, 0, core), col(n, 3, hi), devB, None if light is None else same == light)
+
+    def DETOUR3(n):
+        k, c0, w = COLS[n]
+        light = same
+        src = G[k].at[2 - 2 * light, :, core, :, :, pl.ds(c0, w)]
+        origin = light * hi + (1 - light) * (1 - hi)
+        dev = (1 - dp, o, 2 * (light * hiB + (1 - light) * hiA) + core)
+        send(("y3", n), src, G[k].at[3, :, origin, :, :, pl.ds(c0, w)], dev)
 
     def Y3(n):
         here = col(n, 3, hiA)
@@ -155,63 +168,57 @@
             h, p = b // 2, b % 2
             for c in range(3):
                 piece[(h + p) % 2, :, c * 256 + h * 128:c * 256 + h * 128 + 128] = FT[h, rows, c * 256 + p * 128:c * 256 + p * 128 + 128]
-        for p in (0, 1):
-            send(("fp", p), piece.at[p], rows_of(p, o), partner)
+
+    def pair(j):
+        return p1 if j == 0 else 1 - p1
+
+    def pieces(j):
+        p = 1 - pair(j)
+        send(("fp", j), piece.at[p], rows_of(p, o), partner)
 
     def rows_of(p, out, first=0, n=96):
         return FTo.at[p, pl.ds(pl.multiple_of(out * 96 + first, 16), n), :]
 
-    def on(p, da, db):
-        return at(x + da, z + db) if p == 0 else at(x + db, z + da)
-
-    def to(p, da, db):
-        return (dp, on(p, da, db), i)
-
-    def F0():
-        for p in (0, 1):
-            here = rows_of(p, o)
-            got(("fp", p), here)
-            send(("f1", p, 0), here, here, to(p, 1, 0))
-            send(("f1", p, 1), here, here, to(p, -1, 0))
+    def rows_at(j, dz, dx, first=0, n=96):
+        return rows_of(pair(j), at(x + dx, z + dz), first, n)
+
+    def F0(j):
+        here = rows_at(j, 0, 0)
+        got(("fp", j), here)
+        send(("f1", j, 0), here, here, plane(x, z + 1))
+        send(("f1", j, 1), here, here, plane(x, z - 1))
 
     OFF = (0, -1, 1, 2)
 
-    def spread(p, k):
-        here = rows_of(p, on(p, OFF[k], 0))
-        send(("f2", p, k, 0), here, here, to(p, 0, 1))
-        send(("f2", p, k, 1), here, here, to(p, 0, -1))
-
-    def F1():
-        for p in (0, 1):
-            got(("f1", p, 0), rows_of(p, on(p, -1, 0)))
-            half = rows_of(p, on(p, -1, 0), 0, 48)
-            send(("f1", p, 2), half, half, to(p, 1, 0))
-            got(("f1", p, 1), rows_of(p, on(p, 1, 0)))
-            half = rows_of(p, on(p, 1, 0), 48, 48)
-            send(("f1", p, 3), half, half, to(p, -1, 0))
-        for k in (0, 1, 2):
-            for p in (0, 1):
-                spread(p, k)
-
-    def F2():
-        for p in (0, 1):
-            got(("f1", p, 2), rows_of(p, on(p, 2, 0), 0, 48))
-            got(("f1", p, 3), rows_of(p, on(p, 2, 0), 48, 48))
-            spread(p, 3)
-
-    def F3(k):
-        for p in (0, 1):
-            side = 0 if k < 2 else 1
-            here = rows_of(p, on(p, OFF[k], -1 if side == 0 else 1))
-            got(("f2", p, k, side), here)
-            send(("f3", p, k), here, here, to(p, 0, 1 if side == 0 else -1))
-
-    def F4():
-        for p in (0, 1):
-            for k in range(4):
-                side = 1 if k < 2 else 0
-                got(("f2", p, k, side), rows_of(p, on(p, OFF[k], -1 if side == 0 else 1)))
-                got(("f3", p, k), rows_of(p, on(p, OFF[k], 2)))
+    def spread(j, k):
+        here = rows_at(j, OFF[k], 0)
+        send(("f2", j, k, 0), here, here, plane(x + 1, z))
+        send(("f2", j, k, 1), here, here, plane(x - 1, z))
+
+    def F1(j):
+        got(("f1", j, 0), rows_at(j, -1, 0))
+        half = rows_at(j, -1, 0, 0, 48)
+        send(("f1", j, 2), half, half, plane(x, z + 1))
+        got(("f1", j, 1), rows_at(j, 1, 0))
+        half = rows_at(j, 1, 0, 48, 48)
+        send(("f1", j, 3), half, half, plane(x, z - 1))
+
+    def F2(j):
+        got(("f1", j, 2), rows_at(j, 2, 0, 0, 48))
+        got(("f1", j, 3), rows_at(j, 2, 0, 48, 48))
+        spread(j, 3)
+
+    def F3(j, k):
+        side = 0 if k < 2 else 1
+        here = rows_at(j, OFF[k], -1 if side == 0 else 1)
+        got(("f2", j, k, side), here)
+        send(("f3", j, k), here, here, plane(x + (1 if side == 0 else -1), z))
+
+    def F4(j):
+        for k in range(4):
+            side = 1 if k < 2 else 0
+            got(("f2", j, k, side), rows_at(j, OFF[k], -1 if side == 0 else 1))
+            got(("f3", j, k), rows_at(j, OFF[k], 2))
 
     def GF(s, c):
         slot = 2 * s
@@ -265,131 +272,176 @@
             got(("r4", s, c), rx2.at[s, c])
             gout[c] = (Pp[s, c, keep, z].astype(F32) + rx2[s, c].astype(F32)).astype(BF)
 
-    def PASS(slot, n):
-        k, c0, w = COLS[n]
+    def PASS(slot, n, c0=0, c1=3):
+        k, first, w = COLS[n]
         f = (FT.at[hi], FTo.at[p1], FT.at[1 - hi], FTo.at[1 - p1])[slot]
         acc = ACC[k]
-        step = min(w, 256)
-
-        def body(j, carry):
-            cs = pl.ds(pl.multiple_of(c0 + j * step, 128), step)
-            g = G[k][slot, :, :, :, :, cs].reshape(768, step)
-            r = jnp.dot(f[...], g, preferred_element_type=F32)
+        cs = pl.ds(first, w)
+        g = G[k][slot, c0:c1, :, :, :, cs].reshape((c1 - c0) * 256, w)
+        half = F if w > 256 else F // 2
+        for m in range(0, F, half):
+            ms = pl.ds(m, half)
+            r = jnp.dot(f[ms, c0 * 256:c1 * 256], g, preferred_element_type=F32)
             if slot == 0:
-                acc[:, cs] = r
+                acc[ms, cs] = r
             elif slot < 3:
-                acc[:, cs] += r
+                acc[ms, cs] += r
             else:
-                W[k][:, cs] = (acc[:, cs] + r).astype(BF)
-            return carry
-
-        lax.fori_loop(0, w // step, body, 0)
+                W[k][ms, cs] = (acc[ms, cs] + r).astype(BF)
         if slot == 3:
-            local(("o", n), W[k].at[:, pl.ds(c0, w)], OUT[k].at[:, pl.ds(c0, w)])
-
-    own_q(0)
-    own_m(0)
-    own_q(1)
+            local(("o", n), W[k].at[:, cs], OUT[k].at[:, cs])
+
+    def result():
+        for c in range(3):
+            local(("gf", c), gout.at[c], gf_out.at[c])
+
+    def loaded():
+        for c in range(3):
+            lwait["q", c].wait()
+        lwait["wq",].wait()
+        lwait["wm",].wait()
+
     transpose()
-    own_m(1)
-    own_q(2)
-    own_m(2)
-    for c in range(3):
-        lwait["q", c].wait()
-    lwait["wq",].wait()
-    lwait["wm",].wait()
+    slope(0)
+    friends_here()
+    pieces(0)
+    pieces(1)
+    own(0)
+    sib_q(0)
+    sib_m(0)
+    sib_q(1)
+    sib_q(2)
+    slope(1)
+    sib_m(1)
+    slope(2)
+    sib_m(2)
+    loaded()
     SIB(0, 0)
     GF(0, 0)
-    F0()
-    Y1(0)
+    own(1)
     SIB(0, 1)
     GF(0, 1)
-    F1()
+    F0(0)
+    spread(0, 0)
     SIB(0, 2)
     GF(0, 2)
-    F2()
+    own(2)
     PASS(0, 0)
-    Y1(1)
-    R1(0, 0)
+    F1(0)
+    spread(0, 1)
+    spread(0, 2)
+    F0(1)
     PASS(0, 1)
     PASS(0, 2)
-    F3(0)
+    PASS(0, 3)
+    F2(0)
+    Y1(0)
+    PASS(0, 4)
+    F1(1)
+    PASS(0, 5)
+    R1(0, 0)
     R1(0, 1)
-    PASS(0, 3)
+    R1(0, 2)
+    F3(0, 0)
+    F3(0, 1)
+    Y1(1)
+    F3(0, 2)
+    F3(0, 3)
     R2(0, 0)
-    F3(1)
-    PASS(0, 4)
-    F3(2)
-    R1(0, 2)
+    Y1(2)
+    spread(1, 0)
     R2(0, 1)
-    PASS(0, 5)
-    Y1(2)
-    F3(3)
-    R3(0, 0)
+    spread(1, 1)
     R2(0, 2)
+    spread(1, 2)
+    F2(1)
+    SIB(1, 0)
+    SIB(1, 1)
+    SIB(1, 2)
+    F4(0)
+    PASS(1, 0)
+    PASS(1, 1)
     Y2(0)
-    R3(0, 1)
-    R4(0, 0)
+    PASS(1, 2)
     SIB(2, 0)
     GF(1, 0)
     R1(1, 0)
-    R3(0, 2)
-    R4(0, 1)
-    R5(0, 0)
-    SEND3(0)
+    F3(1, 0)
+    R3(0, 0)
+    PASS(1, 3)
     Y2(1)
-    R4(0, 2)
-    R5(0, 1)
+    SEND3(0, 1)
+    SEND3(1, 1)
+    PASS(1, 4)
     SIB(2, 1)
     GF(1, 1)
     R1(1, 1)
     R2(1, 0)
-    SEND3(1)
+    F3(1, 1)
+    R3(0, 1)
+    PASS(1, 5)
+    F3(1, 2)
+    Y2(2)
+    SEND3(0, 0)
+    SEND3(1, 0)
     SEND3(2)
-    R5(0, 2)
-    Y2(2)
-    for n in (3, 4, 5):
-        SEND3(n)
+    SEND3(3)
+    PASS(2, 0, 0, 2)
     SIB(2, 2)
     GF(1, 2)
     R1(1, 2)
     R2(1, 1)
+    SEND3(4)
+    DETOUR3(5)
+    F3(1, 3)
+    PASS(2, 1, 0, 2)
+    Y3(0)
     R3(1, 0)
-    PASS(2, 0)
-    PASS(2, 1)
+    PASS(2, 2, 0, 2)
+    PASS(2, 3, 0, 2)
+    R3(0, 2)
+    R4(0, 0)
+    Y3(1)
+    PASS(2, 4, 0, 2)
+    PASS(2, 5, 0, 2)
     R2(1, 2)
+    Y3(2)
+    PASS(2, 0, 2, 3)
+    PASS(2, 1, 2, 3)
+    PASS(2, 2, 2, 3)
+    R4(1, 0)
+    PASS(2, 3, 2, 3)
+    PASS(2, 4, 2, 3)
+    R4(0, 1)
+    PASS(2, 5, 2, 3)
     R3(1, 1)
-    R4(1, 0)
-    PASS(2, 2)
-    PASS(2, 3)
+    F4(1)
+    SIB3(0)
+    PASS(3, 0)
+    Y3(3)
+    SIB3(1)
+    PASS(3, 1)
+    SIB3(2)
+    PASS(3, 2)
     R3(1, 2)
     R4(1, 1)
+    R4(0, 2)
+    R5(0, 0)
+    SIB3(3)
+    PASS(3, 3)
+    Y3(4)
+    R5(0, 1)
     R5(1, 0)
-    Y3(0)
-    PASS(2, 4)
-    PASS(2, 5)
+    SIB3(4)
+    PASS(3, 4)
     R4(1, 2)
+    Y3(5)
     R5(1, 1)
-    Y3(1)
-    F4()
-    for c in range(3):
-        SIB(1, c)
-    PASS(1, 0)
+    R5(0, 2)
+    SIB3(5)
+    PASS(3, 5)
     R5(1, 2)
-    for c in range(3):
-        local(("gf", c), gout.at[c], gf_out.at[c])
-    PASS(1, 1)
-    Y3(2)
-    PASS(1, 2)
-    PASS(1, 3)
-    Y3(3)
-    PASS(1, 4)
-    PASS(1, 5)
-    for n in range(6):
-        if n >= 4:
-            Y3(n)
-        SIB3(n)
-        PASS(3, n)
+    result()
     for n in range(6):
         lwait["o", n].wait()
     for c in range(3):
@@ -399,6 +451,23 @@
             c.wait_send()
         else:
             pl.when(when)(c.wait_send)
+
+
+def copy_out(a, b, c, x, y, z, va, vb, vc, sem):
+    parts = []
+    for src, mid, dst, n in ((b, vb, y, 4), (c, vc, z, 4), (a, va, x, 1)):
+        rows = src.shape[0] // n
+        for j in range(n):
+            r = pl.ds(j * rows, rows)
+            i = len(parts)
+            parts.append((pltpu.make_async_copy(src.at[r], mid.at[r], sem.at[0, i]), pltpu.make_async_copy(mid.at[r], dst.at[r], sem.at[1, i])))
+    for load, _ in parts:
+        load.start()
+    for load, store in parts:
+        load.wait()
+        store.start()
+    for _, store in parts:
+        store.wait()
 
 
 def local(features, grad_qkv, grad_act, preact, w_qkv, w_mlp):
@@ -441,7 +510,17 @@
         w_qkv,
         w_mlp,
     )
-    return gf.reshape(96, F), gwq, gwm
+    gf = gf.reshape(96, F)
+    return pl.pallas_call(
+        copy_out,
+        name="results",
+        out_shape=tuple(shape(v.shape, BF) for v in (gf, gwq, gwm)),
+        in_specs=[pl.BlockSpec(memory_space=pl.ANY)] * 3,
+        out_specs=(pl.BlockSpec(memory_space=pl.ANY),) * 3,
+        scratch_shapes=[vm(v.shape, BF) for v in (gf, gwq, gwm)] + [pltpu.SemaphoreType.DMA((2, 9))],
+        compiler_params=pltpu.CompilerParams(vmem_limit_bytes=60 * 2**20),
+        cost_estimate=pl.CostEstimate(flops=0, bytes_accessed=17_000_000, transcendentals=0),
+    )(gf, gwq, gwm)
 
 
 def solution(mesh):

time: 131 us -> 96.9 us (0.74)
  Pallas kernels: 122 us -> 95.5 us
  local copies, waits for them, and re-layouts: 8.1 us -> 0 us
    pallas_call x1, Pallas kernels: 122 us -> 89.1 us  [local(): pl.pallas_call(kernel, name='joined_projection_backward', out_shape=(shap...]
    unnamed x5 -> x0, local copies, waits for them, and re-layouts: 8.1 us -> none
    pallas_call x0 -> x1, Pallas kernels: none -> 6.39 us  [local(): pl.pallas_call(copy_out, name='results', out_shape=tuple((shape(v.shape,...]
where the time goes in v2:
time: 96.9 us; the launch traced here: 96.4 us
  Pallas kernels  95.5 us (99%)
    pallas_call x1, Pallas kernels, local(): pl.pallas_call(kernel, name='joined_projection_backward', out_shape=(shap...  89.1 us
    pallas_call x1, Pallas kernels, local(): pl.pallas_call(copy_out, name='results', out_shape=tuple((shape(v.shape,...  6.39 us

profile of v2, /device:TPU:16, one launch (start us, length us, event | category | flops | bytes accessed | tf_op | source)
XLA Modules:
  0.0 96.4 jit_solution(1386382237156148947)
XLA Ops:
  0.6 89.1 %joined_projection_backward.1 = (bf16[3,32,1536]{2,1,0:T(8,128)(2,1)}, bf16[1536,1152]{1,0:T(8,128)(2,1)}, bf16[1536,1536]{1,0:T(8,128)(2,1)}) custom-call(bf16[4,4,3,32,1536]{4,3,2,1,0:T(8,128)(2,1)} %bitcast.6, bf16[4,3,32,1152]{3,2,1,0:T(8,128)(2,1)} %bitcast.9, bf16[4,3,32,1536]{3,2,1,0:T(8,128)(2,1)} %bitcast.7, bf16[4,3,32,1536]{3,2,1,0:T(8,128)(2,1)} %bitcast.8, ...), custom_call_target="tpu_custom_call" | custom-call | flops 38000001024 | bytes 25000000 | tf_op jit(solution)/shard_map/joined_projection_backward/pallas_call | solution.py:476
  89.8 6.4 %results.1 = (bf16[96,1536]{1,0:T(8,128)(2,1)}, bf16[1536,1152]{1,0:T(8,128)(2,1)}, bf16[1536,1536]{1,0:T(8,128)(2,1)}) custom-call(bf16[96,1536]{1,0:T(8,128)(2,1)} %bitcast.5, bf16[1536,1152]{1,0:T(8,128)(2,1)} %get-tuple-element.7.b, bf16[1536,1536]{1,0:T(8,128)(2,1)} %get-tuple-element.8.c), custom_call_target="tpu_custom_call" | custom-call | bytes 17000000 | tf_op jit(solution)/shard_map/results/pallas_call | solution.py:514

commit v3 on v2

--- a/solution.py
+++ b/solution.py
@@ -65,8 +65,8 @@
     lids = {}
     lwait = {}
 
-    def local(key, src, dst):
-        n = lids.setdefault(key, len(lids))
+    def local(key, src, dst, after=None):
+        n = lids[after] if after else lids.setdefault(key, len(lids))
         c = pltpu.make_async_copy(src, dst, lsem.at[n])
         c.start()
         lwait[key] = c
@@ -74,7 +74,7 @@
     for b in range(4):
         for c in range(3):
             local(("f", b, c), feat.at[b, :, c], Pp.at[b // 2, c, b % 2])
-    for c in range(3):
+    for c in range(2):
         local(("ga", c), ga.at[:, c], stg.at[0, c])
         local(("pre", c), pre.at[:, c], stg.at[1, c])
     for c in range(3):
@@ -105,12 +105,15 @@
         lwait["pre", c].wait()
 
         def body(j, carry):
-            a = stg[0, c, j].astype(F32)
-            v = stg[1, c, j].astype(F32)
+            a = stg[0, c % 2, j].astype(F32)
+            v = stg[1, c % 2, j].astype(F32)
             Gm[0, c, core, j] = (a * gelu_slope(v)).astype(BF)
             return carry
 
         lax.fori_loop(0, 4, body, 0)
+        if c == 0:
+            local(("ga", 2), ga.at[:, 2], stg.at[0, 0], ("ga", 0))
+            local(("pre", 2), pre.at[:, 2], stg.at[1, 0], ("pre", 0))
 
     def sib_m(c):
         send(("s0", 1, c), tok(1, 0, c, core), tok(1, 0, c, core), sib)
@@ -140,17 +143,26 @@
     def SEND3(n, light=None):
         send(("y3", n), col(n, 0, core), col(n, 3, hi), devB, None if light is None else same == light)
 
+    PARTS = (pl.ds(0, 2), pl.ds(2, 1))
+
+    def part(n, j, slot, pos):
+        k, c0, w = COLS[n]
+        return G[k].at[slot, PARTS[j], pos, :, :, pl.ds(c0, w)]
+
     def DETOUR3(n):
-        k, c0, w = COLS[n]
         light = same
-        src = G[k].at[2 - 2 * light, :, core, :, :, pl.ds(c0, w)]
         origin = light * hi + (1 - light) * (1 - hi)
         dev = (1 - dp, o, 2 * (light * hiB + (1 - light) * hiA) + core)
-        send(("y3", n), src, G[k].at[3, :, origin, :, :, pl.ds(c0, w)], dev)
+        send(("y3", n, 0), part(n, 0, 2 - 2 * light, core), part(n, 0, 3, origin), dev)
+        send(("y3", n, 1), part(n, 1, 0, core), part(n, 1, 3, hi), devB)
 
     def Y3(n):
         here = col(n, 3, hiA)
-        got(("y3", n), here)
+        if n == 5:
+            for j in (0, 1):
+                got(("y3", n, j), part(n, j, 3, hiA))
+        else:
+            got(("y3", n), here)
         send(("s3", n), here, here, sib)
 
     def SIB3(n):
@@ -222,6 +234,8 @@
 
     def GF(s, c):
         slot = 2 * s
+        if s == 1:
+            SIB(2, c)
         a = Gq[slot, c].reshape(256, NQ)
         b = Gm[slot, c].reshape(256, NM)
         r = lax.dot_general(a, Wq[...], (((1,), (1,)), ((), ())), preferred_element_type=F32)
@@ -238,39 +252,47 @@
         keep = jnp.where(is_d, odd, 1 - odd)
         return is_d, odd, keep
 
-    def R1(s, c):
-        send(("r1", s, c, 0), Pp.at[s, c, :, z2, :, A], ra.at[s, c, 0], plane(x, z + 1))
-        send(("r1", s, c, 1), Pp.at[s, c, :, z2, :, B], ra.at[s, c, 1], plane(x, z - 1))
-
-    def R2(s, c):
-        got(("r1", s, c, 0), ra.at[s, c, 0])
-        Pp[s, c, :, zr, :, 0:768] = (Pp[s, c, :, zr, :, 0:768].astype(F32) + ra[s, c, 0].astype(F32)).astype(BF)
-        send(("r2", s, c, 0), Pp.at[s, c, :, zr], rb.at[s, c, 0], plane(x, z + 1))
-        got(("r1", s, c, 1), ra.at[s, c, 1])
-        Pp[s, c, :, zl, :, 768:1536] = (Pp[s, c, :, zl, :, 768:1536].astype(F32) + ra[s, c, 1].astype(F32)).astype(BF)
-        send(("r2", s, c, 1), Pp.at[s, c, :, zl], rb.at[s, c, 1], plane(x, z - 1))
-
-    def R3(s, c):
+    def rows(j):
+        return pl.ds(0, 32) if j is None else pl.ds(16 * j, 16)
+
+    def R1(s, c, j=None):
+        r = rows(j)
+        send(("r1", s, c, j, 0), Pp.at[s, c, :, z2, r, A], ra.at[s, c, 0, :, r], plane(x, z + 1))
+        send(("r1", s, c, j, 1), Pp.at[s, c, :, z2, r, B], ra.at[s, c, 1, :, r], plane(x, z - 1))
+
+    def R2(s, c, j=None):
+        r = rows(j)
+        got(("r1", s, c, j, 0), ra.at[s, c, 0, :, r])
+        Pp[s, c, :, zr, r, 0:768] = (Pp[s, c, :, zr, r, 0:768].astype(F32) + ra[s, c, 0, :, r].astype(F32)).astype(BF)
+        send(("r2", s, c, j, 0), Pp.at[s, c, :, zr, r], rb.at[s, c, 0, :, r], plane(x, z + 1))
+        got(("r1", s, c, j, 1), ra.at[s, c, 1, :, r])
+        Pp[s, c, :, zl, r, 768:1536] = (Pp[s, c, :, zl, r, 768:1536].astype(F32) + ra[s, c, 1, :, r].astype(F32)).astype(BF)
+        send(("r2", s, c, j, 1), Pp.at[s, c, :, zl, r], rb.at[s, c, 1, :, r], plane(x, z - 1))
+
+    def R3(s, c, j=None):
+        r = rows(j)
         is_d, odd, keep = role(s)
-        got(("r2", s, c, 0), rb.at[s, c, 0])
-        got(("r2", s, c, 1), rb.at[s, c, 1])
-        v = Pp[s, c, :, z].astype(F32) + rb[s, c, 0].astype(F32) + rb[s, c, 1].astype(F32)
-        Pp[s, c, :, z] = v.astype(BF)
-        send(("r3", s, c), Pp.at[s, c, 1 - keep, z], rx1.at[s, c], plane(x + 1 - 2 * odd, z))
-
-    def R4(s, c):
+        got(("r2", s, c, j, 0), rb.at[s, c, 0, :, r])
+        got(("r2", s, c, j, 1), rb.at[s, c, 1, :, r])
+        v = Pp[s, c, :, z, r].astype(F32) + rb[s, c, 0, :, r].astype(F32) + rb[s, c, 1, :, r].astype(F32)
+        Pp[s, c, :, z, r] = v.astype(BF)
+        send(("r3", s, c, j), Pp.at[s, c, 1 - keep, z, r], rx1.at[s, c, r], plane(x + 1 - 2 * odd, z))
+
+    def R4(s, c, j=None):
+        r = rows(j)
         is_d, odd, keep = role(s)
-        got(("r3", s, c), rx1.at[s, c])
-        Pp[s, c, keep, z] = (Pp[s, c, keep, z].astype(F32) + rx1[s, c].astype(F32)).astype(BF)
-        send(("r4", s, c), Pp.at[s, c, keep, z], rx2.at[s, c], plane(x - 1 + 2 * odd, z), when=jnp.logical_not(is_d))
-
-    def R5(s, c):
+        got(("r3", s, c, j), rx1.at[s, c, r])
+        Pp[s, c, keep, z, r] = (Pp[s, c, keep, z, r].astype(F32) + rx1[s, c, r].astype(F32)).astype(BF)
+        send(("r4", s, c, j), Pp.at[s, c, keep, z, r], rx2.at[s, c, r], plane(x - 1 + 2 * odd, z), when=jnp.logical_not(is_d))
+
+    def R5(s, c, j=None):
+        r = rows(j)
         is_d, odd, keep = role(s)
 
         @pl.when(is_d)
         def _():
-            got(("r4", s, c), rx2.at[s, c])
-            gout[c] = (Pp[s, c, keep, z].astype(F32) + rx2[s, c].astype(F32)).astype(BF)
+            got(("r4", s, c, j), rx2.at[s, c, r])
+            gout[c, r] = (Pp[s, c, keep, z, r].astype(F32) + rx2[s, c, r].astype(F32)).astype(BF)
 
     def PASS(slot, n, c0=0, c1=3):
         k, first, w = COLS[n]
@@ -289,11 +311,21 @@
             else:
                 W[k][ms, cs] = (acc[ms, cs] + r).astype(BF)
         if slot == 3:
-            local(("o", n), W[k].at[:, cs], OUT[k].at[:, cs])
-
-    def result():
-        for c in range(3):
-            local(("gf", c), gout.at[c], gf_out.at[c])
+            local(("o", n), W[k].at[:, cs], OUT[k].at[:, cs], ("f", n // 3, n % 3))
+
+    def PASSM(c0, c1):
+        def body(n, carry):
+            cs = pl.ds(pl.multiple_of(n * 512, 512), 512)
+            g = Gm[2, c0:c1, :, :, :, cs].reshape((c1 - c0) * 256, 512)
+            for m in (0, 768):
+                ms = pl.ds(m, 768)
+                am[ms, cs] += jnp.dot(FT[1 - hi, ms, c0 * 256:c1 * 256], g, preferred_element_type=F32)
+            return carry
+
+        lax.fori_loop(0, 3, body, 0)
+
+    def result(c):
+        local(("gf", c), gout.at[c], gf_out.at[c], ("f", 2, c))
 
     def loaded():
         for c in range(3):
@@ -361,87 +393,91 @@
     F4(0)
     PASS(1, 0)
     PASS(1, 1)
+    PASS(1, 2)
+    PASS(1, 3)
     Y2(0)
-    PASS(1, 2)
-    SIB(2, 0)
+    PASS(1, 4)
     GF(1, 0)
     R1(1, 0)
     F3(1, 0)
     R3(0, 0)
-    PASS(1, 3)
+    SEND3(0, 1)
+    PASS(1, 5)
     Y2(1)
-    SEND3(0, 1)
     SEND3(1, 1)
-    PASS(1, 4)
-    SIB(2, 1)
+    PASS(2, 0, 0, 1)
+    PASS(2, 1, 0, 1)
+    PASS(2, 2, 0, 1)
     GF(1, 1)
     R1(1, 1)
     R2(1, 0)
     F3(1, 1)
     R3(0, 1)
-    PASS(1, 5)
+    PASSM(0, 1)
     F3(1, 2)
+    SEND3(3, 1)
     Y2(2)
     SEND3(0, 0)
     SEND3(1, 0)
+    SEND3(3, 0)
+    SEND3(4)
+    PASS(2, 0, 1, 2)
+    PASS(2, 1, 1, 2)
+    PASS(2, 2, 1, 2)
+    GF(1, 2)
+    R1(1, 2, 0)
+    R1(1, 2, 1)
+    R2(1, 1)
+    DETOUR3(5)
     SEND3(2)
-    SEND3(3)
-    PASS(2, 0, 0, 2)
-    SIB(2, 2)
-    GF(1, 2)
-    R1(1, 2)
-    R2(1, 1)
-    SEND3(4)
-    DETOUR3(5)
     F3(1, 3)
-    PASS(2, 1, 0, 2)
+    R3(0, 2)
+    PASSM(1, 3)
     Y3(0)
+    R2(1, 2, 0)
     R3(1, 0)
-    PASS(2, 2, 0, 2)
-    PASS(2, 3, 0, 2)
-    R3(0, 2)
     R4(0, 0)
-    Y3(1)
-    PASS(2, 4, 0, 2)
-    PASS(2, 5, 0, 2)
-    R2(1, 2)
-    Y3(2)
     PASS(2, 0, 2, 3)
+    R2(1, 2, 1)
     PASS(2, 1, 2, 3)
     PASS(2, 2, 2, 3)
-    R4(1, 0)
-    PASS(2, 3, 2, 3)
-    PASS(2, 4, 2, 3)
-    R4(0, 1)
-    PASS(2, 5, 2, 3)
-    R3(1, 1)
+    Y3(1)
     F4(1)
     SIB3(0)
     PASS(3, 0)
-    Y3(3)
     SIB3(1)
     PASS(3, 1)
-    SIB3(2)
-    PASS(3, 2)
-    R3(1, 2)
-    R4(1, 1)
-    R4(0, 2)
+    R3(1, 1)
+    R4(1, 0)
+    R4(0, 1)
+    Y3(3)
+    R3(1, 2, 0)
     R5(0, 0)
     SIB3(3)
     PASS(3, 3)
+    R3(1, 2, 1)
     Y3(4)
-    R5(0, 1)
-    R5(1, 0)
+    R4(1, 1)
+    R4(0, 2)
+    R4(1, 2, 0)
+    Y3(5)
     SIB3(4)
     PASS(3, 4)
-    R4(1, 2)
-    Y3(5)
-    R5(1, 1)
-    R5(0, 2)
+    R4(1, 2, 1)
+    R5(1, 0)
+    R5(0, 1)
+    Y3(2)
     SIB3(5)
     PASS(3, 5)
-    R5(1, 2)
-    result()
+    R5(0, 2)
+    result(0)
+    R5(1, 1)
+    result(1)
+    SIB3(2)
+    PASS(3, 2)
+    R5(1, 2, 0)
+    R5(1, 2, 1)
+    result(2)
     for n in range(6):
         lwait["o", n].wait()
     for c in range(3):
@@ -492,13 +528,13 @@
             vm((2, 3, 32, F), BF),
             vm((2, 3, 32, F), BF),
             vm((2, 96, 768), BF),
-            vm((2, 3, 4, 32, NM), BF),
+            vm((2, 2, 4, 32, NM), BF),
             vm((3, 32, F), BF),
             vm((F, NQ), F32),
             vm((F, NM), F32),
-            pltpu.SemaphoreType.DMA((112,)),
-            pltpu.SemaphoreType.DMA((112,)),
-            pltpu.SemaphoreType.DMA((32,)),
+            pltpu.SemaphoreType.DMA((119,)),
+            pltpu.SemaphoreType.DMA((119,)),
+            pltpu.SemaphoreType.DMA((21,)),
         ],
         compiler_params=pltpu.CompilerParams(collective_id=0, has_side_effects=True, vmem_limit_bytes=64 * 2**20 - 2**16),
         cost_estimate=pl.CostEstimate(flops=38_000_000_000, bytes_accessed=25_000_000, transcendentals=1_200_000),

time: 96.9 us -> 93.9 us (0.969)
  Pallas kernels: 95.5 us -> 93 us
    pallas_call x1, Pallas kernels: 89.1 us -> 86.6 us  [local(): pl.pallas_call(kernel, name='joined_projection_backward', out_shape=(shap...]
where the time goes in v3:
time: 93.9 us; the launch traced here: 93.8 us
  Pallas kernels  93 us (99%)
    pallas_call x1, Pallas kernels, local(): pl.pallas_call(kernel, name='joined_projection_backward', out_shape=(shap...  86.6 us
    pallas_call x1, Pallas kernels, local(): pl.pallas_call(copy_out, name='results', out_shape=tuple((shape(v.shape,...  6.39 us

profile of v3, /device:TPU:16, one launch (start us, length us, event | category | flops | bytes accessed | tf_op | source)
XLA Modules:
  0.0 93.8 jit_solution(12709432071587783001)
XLA Ops:
  0.6 86.6 %joined_projection_backward.1 = (bf16[3,32,1536]{2,1,0:T(8,128)(2,1)}, bf16[1536,1152]{1,0:T(8,128)(2,1)}, bf16[1536,1536]{1,0:T(8,128)(2,1)}) custom-call(bf16[4,4,3,32,1536]{4,3,2,1,0:T(8,128)(2,1)} %bitcast.6, bf16[4,3,32,1152]{3,2,1,0:T(8,128)(2,1)} %bitcast.9, bf16[4,3,32,1536]{3,2,1,0:T(8,128)(2,1)} %bitcast.7, bf16[4,3,32,1536]{3,2,1,0:T(8,128)(2,1)} %bitcast.8, ...), custom_call_target="tpu_custom_call" | custom-call | flops 38000001024 | bytes 25000000 | tf_op jit(solution)/shard_map/joined_projection_backward/pallas_call | solution.py:512
  87.2 6.4 %results.1 = (bf16[96,1536]{1,0:T(8,128)(2,1)}, bf16[1536,1152]{1,0:T(8,128)(2,1)}, bf16[1536,1536]{1,0:T(8,128)(2,1)}) custom-call(bf16[96,1536]{1,0:T(8,128)(2,1)} %bitcast.5, bf16[1536,1152]{1,0:T(8,128)(2,1)} %get-tuple-element.7.b, bf16[1536,1536]{1,0:T(8,128)(2,1)} %get-tuple-element.8.c), custom_call_target="tpu_custom_call" | custom-call | bytes 17000000 | tf_op jit(solution)/shard_map/results/pallas_call | solution.py:550

commit v4 on v3

--- a/solution.py
+++ b/solution.py
@@ -461,9 +461,9 @@
     R4(0, 2)
     R4(1, 2, 0)
     Y3(5)
+    R4(1, 2, 1)
     SIB3(4)
     PASS(3, 4)
-    R4(1, 2, 1)
     R5(1, 0)
     R5(0, 1)
     Y3(2)

time: 93.9 us -> 94.4 us (level); the launches traced: 93.8 us -> 93.2 us
  no operation moved by 1% of the time
where the time goes in v4:
time: 94.4 us; the launch traced here: 93.2 us
  Pallas kernels  92.4 us (98%)
    pallas_call x1, Pallas kernels, local(): pl.pallas_call(kernel, name='joined_projection_backward', out_shape=(shap...  86 us
    pallas_call x1, Pallas kernels, local(): pl.pallas_call(copy_out, name='results', out_shape=tuple((shape(v.shape,...  6.39 us

profile of v4, /device:TPU:16, one launch (start us, length us, event | category | flops | bytes accessed | tf_op | source)
XLA Modules:
  0.0 93.2 jit_solution(7900165490217208325)
XLA Ops:
  0.6 86.0 %joined_projection_backward.1 = (bf16[3,32,1536]{2,1,0:T(8,128)(2,1)}, bf16[1536,1152]{1,0:T(8,128)(2,1)}, bf16[1536,1536]{1,0:T(8,128)(2,1)}) custom-call(bf16[4,4,3,32,1536]{4,3,2,1,0:T(8,128)(2,1)} %bitcast.6, bf16[4,3,32,1152]{3,2,1,0:T(8,128)(2,1)} %bitcast.9, bf16[4,3,32,1536]{3,2,1,0:T(8,128)(2,1)} %bitcast.7, bf16[4,3,32,1536]{3,2,1,0:T(8,128)(2,1)} %bitcast.8, ...), custom_call_target="tpu_custom_call" | custom-call | flops 38000001024 | bytes 25000000 | tf_op jit(solution)/shard_map/joined_projection_backward/pallas_call | solution.py:512
  86.7 6.4 %results.1 = (bf16[96,1536]{1,0:T(8,128)(2,1)}, bf16[1536,1152]{1,0:T(8,128)(2,1)}, bf16[1536,1536]{1,0:T(8,128)(2,1)}) custom-call(bf16[96,1536]{1,0:T(8,128)(2,1)} %bitcast.5, bf16[1536,1152]{1,0:T(8,128)(2,1)} %get-tuple-element.7.b, bf16[1536,1536]{1,0:T(8,128)(2,1)} %get-tuple-element.8.c), custom_call_target="tpu_custom_call" | custom-call | bytes 17000000 | tf_op jit(solution)/shard_map/results/pallas_call | solution.py:550
